TPU v7x, 32 devices: a whole 2x2x4 slice. The times are simulated.
32 devices in a mesh: lon: 16 (over z, x, core), lat: 2 (over y).
Axes of the slice: x: 2, y: 2, z: 4, core: 2. Of those that a mesh axis runs over, the one named last changes fastest.
Arguments:
- increment: float32 [4, 512, 2048], P(None, 'lat', 'lon'), may hold values from -6 to 6
- kappa_x: float32 [4, 512, 2048], P(None, 'lat', 'lon'), may hold values from 0.02 to 0.2
- kappa_y: float32 [4, 512, 2048], P(None, 'lat', 'lon'), may hold values from 0.02 to 0.2
- metric_x: float32 [512, 2048], P('lat', 'lon'), may hold values from 0.5 to 1.5
- metric_y: float32 [512, 2048], P('lat', 'lon'), may hold values from 0.5 to 1.5
- cell_area: float32 [512, 2048], P('lat', 'lon'), may hold values from 1 to 2
- sea_mask: int32 [4, 512, 2048], P(None, 'lat', 'lon'), may hold values 0 or 1
- fold_partner: int32 [2048], P('lon'), may hold values from 0 to 2047, as said below
- norm_factor: float32 [4, 512, 2048], P(None, 'lat', 'lon'), may hold values from 0.5 to 36, as said below
Outputs:
- adjoint_out: float32 [4, 512, 2048], P(None, 'lat', 'lon')
Inputs may be any that keep to these rules, and one draw needn't show every extreme that they name: fold_partner[i] = (c - i) mod 2048 for one c, so fold_partner[fold_partner[i]] = i. `norm_factor`: positive factors.
All inputs are finite; a program needn't handle non-finite values. No bound on the sum of `sea_mask` on one device may be relied on, other than what follows from the above.
Results may differ from a plain program's by a relative error of at most 0.00002.
Values sent between devices are 32-bit elements; how exact they have to be, the bound alone decides.
No kernel may reach another device: no remote copies, remote signals or barrier semaphores. Data moves between devices by JAX's collectives and lax.ppermute only.
A program may use at most 384 MiB of HBM per device.

v0:
```python
import jax
import jax.numpy as jnp
from jax import lax
from jax.sharding import PartitionSpec as P

STEPS = 6


def with_halo(cells, sides, width):
    for axis, dim in sides:
        count = lax.axis_size(axis)
        head = lax.slice_in_dim(cells, 0, width, axis=dim)
        tail = lax.slice_in_dim(cells, cells.shape[dim] - width, cells.shape[dim], axis=dim)
        cells = jnp.concatenate(
            [
                lax.ppermute(tail, axis, [(i, (i + 1) % count) for i in range(count)]),
                cells,
                lax.ppermute(head, axis, [((i + 1) % count, i) for i in range(count)]),
            ],
            axis=dim,
        )
    return cells


def fold_mirror(top_row, targets):
    whole_row = lax.all_gather(top_row, "lon", axis=1, tiled=True)
    return jnp.take(whole_row, targets, axis=1)


def per_device(
    increment, kappa_x, kappa_y, metric_x, metric_y, cell_area, sea_mask, fold_partner, norm_factor
):
    levels, clat_rows, clon_cols = increment.shape
    lat_pos = lax.axis_index("lat")
    is_top = lat_pos == lax.axis_size("lat") - 1
    is_bottom = lat_pos == 0
    top_flag = jnp.where(is_top, 1.0, 0.0).astype(jnp.float32)
    sea_cells = sea_mask.astype(jnp.float32)
    raw_x = kappa_x * metric_x[None] * sea_cells
    raw_y = kappa_y * metric_y[None] * sea_cells
    top_y = raw_y[:, -1, :]
    top_sea = sea_cells[:, -1, :]
    whole_y, whole_sea = (
        lax.all_gather(top_y, "lon", axis=1, tiled=True),
        lax.all_gather(top_sea, "lon", axis=1, tiled=True),
    )
    part_y = jnp.take(whole_y, fold_partner, axis=1)
    part_sea = jnp.take(whole_sea, fold_partner, axis=1)
    coef_fold = 0.5 * (top_y * part_sea + part_y * top_sea) * top_flag
    stacked = jnp.stack([sea_cells, raw_x, raw_y])
    padded = with_halo(stacked, (("lon", 3), ("lat", 2)), 1)
    row_index = jnp.arange(clat_rows + 2, dtype=jnp.int32)
    keep_rim = jnp.where(
        (row_index == clat_rows + 1) & is_top | (row_index == 0) & is_bottom, 0.0, 1.0
    ).astype(jnp.float32)
    padded = padded * keep_rim[None, None, :, None]
    sea_pad = padded[0]
    rawx_pad = padded[1]
    rawy_pad = padded[2]
    coef_east = raw_x * sea_pad[:, 1:-1, 2:]
    coef_west = rawx_pad[:, 1:-1, :-2] * sea_cells
    coef_north = raw_y * sea_pad[:, 2:, 1:-1]
    coef_south = rawy_pad[:, :-2, 1:-1] * sea_cells
    field_now = increment
    for step_index in range(STEPS):
        weighted = field_now / cell_area[None]
        wide_pad = with_halo(weighted, (("lon", 2), ("lat", 1)), 1)
        east_side = wide_pad[:, 1:-1, 2:]
        west_side = wide_pad[:, 1:-1, :-2]
        north_side = wide_pad[:, 2:, 1:-1]
        south_side = wide_pad[:, :-2, 1:-1]
        change = (
            coef_east * (east_side - weighted)
            - coef_west * (weighted - west_side)
            + coef_north * (north_side - weighted)
            - coef_south * (weighted - south_side)
        )
        top_w = weighted[:, -1, :]
        mirror = fold_mirror(top_w, fold_partner)
        change = change.at[:, -1, :].add(coef_fold * (mirror - top_w))
        field_now = field_now + change
    return norm_factor * field_now


def solution(mesh):
    return jax.shard_map(
        per_device,
        mesh=mesh,
        in_specs=(
            P(None, "lat", "lon"),
            P(None, "lat", "lon"),
            P(None, "lat", "lon"),
            P("lat", "lon"),
            P("lat", "lon"),
            P("lat", "lon"),
            P(None, "lat", "lon"),
            P("lon"),
            P(None, "lat", "lon"),
        ),
        out_specs=P(None, "lat", "lon"),
        check_vma=False,
    )
```

profile of v0, /device:TPU:0, one launch (start us, length us, event | category | flops | bytes accessed | tf_op | source)
XLA Modules:
  0.0 390.4 jit_solution(5512881094416505215)
XLA Ops:
  3.9 2.1 fusion.67
  8.8 5.0 %collective-permute-start.1 = (f32[3,4,256,1]{2,1,3,0:T(4,128)S(1)}, f32[3,4,256,1]{2,1,3,0:T(4,128)}, u32[]{:S(2)}, u32[]{:S(2)}) collective-permute-start(f32[3,4,256,1]{2,1,3,0:T(4,128)S(1)} %copy.465), channel_id=1, source_target_pairs={{2,0},{4,2},{6,4},{8,6},{10,8},{12,10},{14,12},{16,14},{18,16},{20... | collective-permute-start | bytes 36872 | tf_op jit(solution)/shard_map/ppermute | solution.py:18
  15.6 4.4 %collective-permute-start.4 = (f32[4,256,1]{2,0,1:T(4,128)}, f32[4,256,1]{2,0,1:T(4,128)S(1)}, u32[]{:S(2)}, u32[]{:S(2)}) collective-permute-start(f32[4,256,1]{2,0,1:T(4,128)} %get-tuple-element.136), channel_id=1, source_target_pairs={{2,0},{4,2},{6,4},{8,6},{10,8},{12,10},{14,12},{16,14},{18,16},{20... | collective-permute-start | bytes 12296 | tf_op jit(solution)/shard_map/ppermute | solution.py:18
  20.8 21.7 %all-gather.1 = f32[4,1,2048]{2,0,1:T(4,128)S(1)} all-gather(f32[4,1,128]{2,0,1:T(4,128)S(1)} %slice.460), channel_id=3, replica_groups=mesh['lon'=16,'lat'=2] {'lon'}, dimensions={2}, use_global_device_ids=true | all-gather | bytes 34816 | tf_op jit(solution)/shard_map/all_gather | solution.py:44
  42.5 17.8 %all-gather = f32[4,1,2048]{2,1,0:T(1,128)S(1)} all-gather(f32[4,1,128]{2,1,0:T(1,128)S(1)} %slice.461), channel_id=2, replica_groups=mesh['lon'=16,'lat'=2] {'lon'}, dimensions={2}, use_global_device_ids=true | all-gather | bytes 34816 | tf_op jit(solution)/shard_map/all_gather | solution.py:45
  60.9 18.7 %all-gather.2 = f32[4,1,2048]{2,0,1:T(4,128)S(1)} all-gather(f32[4,1,128]{2,0,1:T(4,128)S(1)} %slice.462), channel_id=4, replica_groups=mesh['lon'=16,'lat'=2] {'lon'}, dimensions={2}, use_global_device_ids=true | all-gather | bytes 34816 | tf_op jit(solution)/shard_map/all_gather | solution.py:26
  92.4 2.4 collective-permute-done.6
  94.8 5.6 %collective-permute-done.7 = f32[4,1,130]{1,0,2:T(4,128)} collective-permute-done((f32[4,1,130]{1,0,2:T(4,128)}, f32[4,1,130]{1,0,2:T(4,128)}, u32[]{:S(2)}, u32[]{:S(2)}) %collective-permute-start.7) | collective-permute-done | bytes 2112 | tf_op jit(solution)/shard_map/ppermute | solution.py:16
  100.4 2.8 pad_maximum_fusion.50
  105.2 2.1 copy.522
  107.3 5.7 %maximum_multiply_fusion = f32[3,4,258,130]{3,1,2,0:T(4,128)S(1)} fusion(f32[3,4,1,130]{3,1,2,0:T(4,128)S(1)} %collective-permute-done.3, f32[3,4,256,1]{3,1,2,0:T(4,128)S(1)} %copy.467, f32[1,4,256,128]{3,1,2,0:T(4,128)} %bitcast.97, f32[1,4,256,128]{3,1,2,0:T(4,128)} %copy-done.13, f32[1,4,256,128]{3,1,2,0:T(4,128)} %copy-done.12, ...), kind=kLoop, calls=%fused_computation.8 | loop fusion | flops 2817360 | bytes 3220872 | tf_op jit(solution)/shard_map/mul | solution.py:56
  115.1 2.1 fusion.39
  119.0 4.4 %collective-permute-start.8 = (f32[4,256,1]{2,0,1:T(4,128)}, f32[4,256,1]{2,0,1:T(4,128)}, u32[]{:S(2)}, u32[]{:S(2)}) collective-permute-start(f32[4,256,1]{2,0,1:T(4,128)} %get-tuple-element.130), channel_id=1, source_target_pairs={{2,0},{4,2},{6,4},{8,6},{10,8},{12,10},{14,12},{16,14},{18,16},{20... | collective-permute-start | bytes 12296 | tf_op jit(solution)/shard_map/ppermute | solution.py:18
  124.5 6.3 %collective-permute-done.9 = f32[4,256,1]{2,0,1:T(4,128)} collective-permute-done((f32[4,256,1]{2,0,1:T(4,128)}, f32[4,256,1]{2,0,1:T(4,128)}, u32[]{:S(2)}, u32[]{:S(2)}) %collective-permute-start.9) | collective-permute-done | bytes 4128 | tf_op jit(solution)/shard_map/ppermute | solution.py:16
  136.7 20.7 %all-gather.3 = f32[4,1,2048]{2,0,1:T(4,128)S(1)} all-gather(f32[4,1,128]{2,0,1:T(4,128)S(1)} %slice-done), channel_id=5, replica_groups=mesh['lon'=16,'lat'=2] {'lon'}, dimensions={2}, use_global_device_ids=true | all-gather | bytes 34816 | tf_op jit(solution)/shard_map/all_gather | solution.py:26
  161.3 3.0 pad_maximum_fusion.42
  164.3 2.1 copy.523
  166.4 2.0 copy.524
  168.5 2.5 fusion.32
  173.1 4.1 %collective-permute-start.12 = (f32[4,256,1]{2,0,1:T(4,128)}, f32[4,256,1]{2,0,1:T(4,128)}, u32[]{:S(2)}, u32[]{:S(2)}) collective-permute-start(f32[4,256,1]{2,0,1:T(4,128)} %get-tuple-element.128), channel_id=1, source_target_pairs={{2,0},{4,2},{6,4},{8,6},{10,8},{12,10},{14,12},{16,14},{18,16},{20... | collective-permute-start | bytes 12296 | tf_op jit(solution)/shard_map/ppermute | solution.py:18
  178.2 6.3 %collective-permute-done.13 = f32[4,256,1]{2,0,1:T(4,128)} collective-permute-done((f32[4,256,1]{2,0,1:T(4,128)}, f32[4,256,1]{2,0,1:T(4,128)}, u32[]{:S(2)}, u32[]{:S(2)}) %collective-permute-start.13) | collective-permute-done | bytes 4128 | tf_op jit(solution)/shard_map/ppermute | solution.py:16
  190.4 20.2 %all-gather.4 = f32[4,1,2048]{2,0,1:T(4,128)S(1)} all-gather(f32[4,1,128]{2,0,1:T(4,128)S(1)} %slice-done.1), channel_id=6, replica_groups=mesh['lon'=16,'lat'=2] {'lon'}, dimensions={2}, use_global_device_ids=true | all-gather | bytes 34816 | tf_op jit(solution)/shard_map/all_gather | solution.py:26
  213.9 3.1 pad_maximum_fusion.34
  217.0 2.1 copy.525
  219.1 2.0 copy.526
  221.1 2.5 fusion.25
  226.7 4.1 %collective-permute-start.16 = (f32[4,256,1]{2,0,1:T(4,128)}, f32[4,256,1]{2,0,1:T(4,128)}, u32[]{:S(2)}, u32[]{:S(2)}) collective-permute-start(f32[4,256,1]{2,0,1:T(4,128)} %get-tuple-element.126), channel_id=1, source_target_pairs={{2,0},{4,2},{6,4},{8,6},{10,8},{12,10},{14,12},{16,14},{18,16},{20... | collective-permute-start | bytes 12296 | tf_op jit(solution)/shard_map/ppermute | solution.py:18
  231.7 6.4 %collective-permute-done.17 = f32[4,256,1]{2,0,1:T(4,128)} collective-permute-done((f32[4,256,1]{2,0,1:T(4,128)}, f32[4,256,1]{2,0,1:T(4,128)}, u32[]{:S(2)}, u32[]{:S(2)}) %collective-permute-start.17) | collective-permute-done | bytes 4128 | tf_op jit(solution)/shard_map/ppermute | solution.py:16
  243.6 21.8 %all-gather.5 = f32[4,1,2048]{2,0,1:T(4,128)} all-gather(f32[4,1,128]{2,0,1:T(4,128)S(1)} %copy-done.41), channel_id=7, replica_groups=mesh['lon'=16,'lat'=2] {'lon'}, dimensions={2}, use_global_device_ids=true | all-gather | bytes 34816 | tf_op jit(solution)/shard_map/all_gather | solution.py:26
  265.4 2.1 copy.502
  267.5 2.6 gather_fusion.5
  271.6 2.7 pad_maximum_fusion.26
  274.4 2.0 copy.527
  278.5 2.5 fusion.18
  283.6 4.1 %collective-permute-start.20 = (f32[4,256,1]{2,0,1:T(4,128)}, f32[4,256,1]{2,0,1:T(4,128)}, u32[]{:S(2)}, u32[]{:S(2)}) collective-permute-start(f32[4,256,1]{2,0,1:T(4,128)} %get-tuple-element.124), channel_id=1, source_target_pairs={{2,0},{4,2},{6,4},{8,6},{10,8},{12,10},{14,12},{16,14},{18,16},{20... | collective-permute-start | bytes 12296 | tf_op jit(solution)/shard_map/ppermute | solution.py:18
  288.5 6.4 %collective-permute-done.21 = f32[4,256,1]{2,0,1:T(4,128)} collective-permute-done((f32[4,256,1]{2,0,1:T(4,128)}, f32[4,256,1]{2,0,1:T(4,128)}, u32[]{:S(2)}, u32[]{:S(2)}) %collective-permute-start.21) | collective-permute-done | bytes 4128 | tf_op jit(solution)/shard_map/ppermute | solution.py:16
  300.5 21.6 %all-gather.6 = f32[4,1,2048]{2,0,1:T(4,128)} all-gather(f32[4,1,128]{2,0,1:T(4,128)S(1)} %copy-done.42), channel_id=8, replica_groups=mesh['lon'=16,'lat'=2] {'lon'}, dimensions={2}, use_global_device_ids=true | all-gather | bytes 34816 | tf_op jit(solution)/shard_map/all_gather | solution.py:26
  322.1 2.1 copy.509
  324.2 2.6 gather_fusion.6
  328.3 2.7 pad_maximum_fusion.18
  331.0 2.0 copy.529
  335.1 2.5 fusion.11
  340.2 4.1 %collective-permute-start.24 = (f32[4,256,1]{2,0,1:T(4,128)}, f32[4,256,1]{2,0,1:T(4,128)}, u32[]{:S(2)}, u32[]{:S(2)}) collective-permute-start(f32[4,256,1]{2,0,1:T(4,128)} %get-tuple-element.122), channel_id=1, source_target_pairs={{2,0},{4,2},{6,4},{8,6},{10,8},{12,10},{14,12},{16,14},{18,16},{20... | collective-permute-start | bytes 12296 | tf_op jit(solution)/shard_map/ppermute | solution.py:18
  344.6 7.0 %collective-permute-done.25 = f32[4,256,1]{2,0,1:T(4,128)} collective-permute-done((f32[4,256,1]{2,0,1:T(4,128)}, f32[4,256,1]{2,0,1:T(4,128)}, u32[]{:S(2)}, u32[]{:S(2)}) %collective-permute-start.25) | collective-permute-done | bytes 4128 | tf_op jit(solution)/shard_map/ppermute | solution.py:16
  357.1 20.2 %all-gather.7 = f32[4,1,2048]{2,0,1:T(4,128)S(1)} all-gather(f32[4,1,128]{2,0,1:T(4,128)S(1)} %slice.492), channel_id=9, replica_groups=mesh['lon'=16,'lat'=2] {'lon'}, dimensions={2}, use_global_device_ids=true | all-gather | bytes 34816 | tf_op jit(solution)/shard_map/all_gather | solution.py:26
  380.7 2.7 pad_maximum_fusion.10
  384.7 2.1 copy.532
  386.8 2.3 fusion.4
  (234 shorter events, 91.3 us)
Async XLA Ops:
  2.7 17.3 %copy-start = (f32[4,256,128]{2,0,1:T(4,128)}, f32[4,256,128]{2,0,1:T(4,128)S(1)}, u32[]{:S(2)}) copy-start(f32[4,256,128]{2,0,1:T(4,128)S(1)} %get-tuple-element.135) | copy-start | bytes 1572868
  5.9 7.9 %copy-start.8 = (f32[4,256,128]{2,1,0:T(8,128)S(1)}, f32[4,256,128]{2,1,0:T(8,128)}, u32[]{:S(2)}) copy-start(f32[4,256,128]{2,1,0:T(8,128)} %param.23) | copy-start | bytes 1572868
  5.9 7.9 %copy-start.18 = (f32[256,128]{1,0:T(8,128)S(1)}, f32[256,128]{1,0:T(8,128)}, u32[]{:S(2)}) copy-start(f32[256,128]{1,0:T(8,128)} %param.28) | copy-start | bytes 393220
  7.7 79.7 %collective-permute-start = (f32[3,4,256,1]{2,1,3,0:T(4,128)S(1)}, f32[3,4,256,1]{2,1,3,0:T(4,128)S(1)}, u32[]{:S(2)}, u32[]{:S(2)}) collective-permute-start(f32[3,4,256,1]{2,1,3,0:T(4,128)S(1)} %copy.464), channel_id=1, source_target_pairs={{0,2},{2,4},{4,6},{6,8},{8,10},{10,12},{12,14},{14,16},{16,18},{18... | collective-permute-start | bytes 36872 | tf_op jit(solution)/shard_map/ppermute | solution.py:16
  8.8 11.9 %copy-start.46 = (s32[128]{0:T(128)S(1)}, s32[128]{0:T(128)}, u32[]{:S(2)}) copy-start(s32[128]{0:T(128)} %param.30) | copy-start | bytes 1540
  8.8 79.2 %collective-permute-start.1 = (f32[3,4,256,1]{2,1,3,0:T(4,128)S(1)}, f32[3,4,256,1]{2,1,3,0:T(4,128)}, u32[]{:S(2)}, u32[]{:S(2)}) collective-permute-start(f32[3,4,256,1]{2,1,3,0:T(4,128)S(1)} %copy.465), channel_id=1, source_target_pairs={{2,0},{4,2},{6,4},{8,6},{10,8},{12,10},{14,12},{16,14},{18,16},{20... | collective-permute-start | bytes 36872 | tf_op jit(solution)/shard_map/ppermute | solution.py:18
  14.3 65.6 %copy-start.2 = (f32[4,256,128]{2,0,1:T(4,128)}, f32[4,256,128]{2,0,1:T(4,128)S(1)}, u32[]{:S(2)}) copy-start(f32[4,256,128]{2,0,1:T(4,128)S(1)} %copy_divide_fusion) | copy-start | bytes 1572868
  15.6 67.6 %collective-permute-start.5 = (f32[4,256,1]{2,0,1:T(4,128)}, f32[4,256,1]{2,0,1:T(4,128)S(1)}, u32[]{:S(2)}, u32[]{:S(2)}) collective-permute-start(f32[4,256,1]{2,0,1:T(4,128)} %get-tuple-element.137), channel_id=1, source_target_pairs={{0,2},{2,4},{4,6},{6,8},{8,10},{10,12},{12,14},{14,16},{16,18},{18... | collective-permute-start | bytes 12296 | tf_op jit(solution)/shard_map/ppermute | solution.py:16
  15.6 67.8 %collective-permute-start.4 = (f32[4,256,1]{2,0,1:T(4,128)}, f32[4,256,1]{2,0,1:T(4,128)S(1)}, u32[]{:S(2)}, u32[]{:S(2)}) collective-permute-start(f32[4,256,1]{2,0,1:T(4,128)} %get-tuple-element.136), channel_id=1, source_target_pairs={{2,0},{4,2},{6,4},{8,6},{10,8},{12,10},{14,12},{16,14},{18,16},{20... | collective-permute-start | bytes 12296 | tf_op jit(solution)/shard_map/ppermute | solution.py:18
  20.7 202.9 %copy-start.36 = (pred[128]{0:T(512)(128)(4,1)}, pred[128]{0:T(512)(128)(4,1)S(1)}, u32[]{:S(2)}) copy-start(pred[128]{0:T(512)(128)(4,1)S(1)} %compare_and_fusion) | copy-start | bytes 388
  42.5 169.5 %copy-start.39 = (s32[1024]{0:T(1024)}, s32[1024]{0:T(1024)S(1)}, u32[]{:S(2)}) copy-start(s32[1024]{0:T(1024)S(1)} %pad_clamp_fusion) | copy-start | bytes 12292
  79.8 4.3 %copy-start.19 = (f32[4,256,128]{1,0,2:T(4,128)}, f32[4,256,128]{1,0,2:T(4,128)S(1)}, u32[]{:S(2)}) copy-start(f32[4,256,128]{1,0,2:T(4,128)S(1)} %copy.471) | copy-start | bytes 1572868
  84.0 4.1 %copy-start.25 = (f32[4,256,1]{2,0,1:T(4,128)}, f32[4,256,1]{2,0,1:T(4,128)S(1)}, u32[]{:S(2)}) copy-start(f32[4,256,1]{2,0,1:T(4,128)S(1)} %collective-permute-done.4) | copy-start | bytes 12292
  85.3 9.5 %collective-permute-start.6 = (f32[4,1,130]{1,0,2:T(4,128)}, f32[4,1,130]{1,0,2:T(4,128)}, u32[]{:S(2)}, u32[]{:S(2)}) collective-permute-start(f32[4,1,130]{1,0,2:T(4,128)} %get-tuple-element.120), channel_id=1, source_target_pairs={{1,0},{0,1},{3,2},{2,3},{5,4},{4,5},{7,6},{6,7},{9,8},{8,9},{11,10... | collective-permute-start | bytes 6248 | tf_op jit(solution)/shard_map/ppermute | solution.py:18
  87.2 13.2 %collective-permute-start.7 = (f32[4,1,130]{1,0,2:T(4,128)}, f32[4,1,130]{1,0,2:T(4,128)}, u32[]{:S(2)}, u32[]{:S(2)}) collective-permute-start(f32[4,1,130]{1,0,2:T(4,128)} %get-tuple-element.121), channel_id=1, source_target_pairs={{0,1},{1,0},{2,3},{3,2},{4,5},{5,4},{6,7},{7,6},{8,9},{9,8},{10,11... | collective-permute-start | bytes 6248 | tf_op jit(solution)/shard_map/ppermute | solution.py:16
  89.5 10.9 %copy-start.20 = (f32[4,256,128]{1,0,2:T(4,128)S(1)}, f32[4,256,128]{1,0,2:T(4,128)}, u32[]{:S(2)}) copy-start(f32[4,256,128]{1,0,2:T(4,128)} %copy-done.19) | copy-start | bytes 1572868
  90.3 16.9 %collective-permute-start.2 = (f32[3,4,1,130]{3,1,2,0:T(4,128)S(1)}, f32[3,4,1,130]{3,1,2,0:T(4,128)S(1)}, u32[]{:S(2)}, u32[]{:S(2)}) collective-permute-start(f32[3,4,1,130]{3,1,2,0:T(4,128)S(1)} %get-tuple-element.91), channel_id=1, source_target_pairs={{0,1},{1,0},{2,3},{3,2},{4,5},{5,4},{6,7},{7,6},{8,9},{9,8},{10,11... | collective-permute-start | bytes 18728 | tf_op jit(solution)/shard_map/ppermute | solution.py:16
  92.3 15.0 %collective-permute-start.3 = (f32[3,4,1,130]{3,1,2,0:T(4,128)S(1)}, f32[3,4,1,130]{3,1,2,0:T(4,128)S(1)}, u32[]{:S(2)}, u32[]{:S(2)}) collective-permute-start(f32[3,4,1,130]{3,1,2,0:T(4,128)S(1)} %get-tuple-element.92), channel_id=1, source_target_pairs={{1,0},{0,1},{3,2},{2,3},{5,4},{4,5},{7,6},{6,7},{9,8},{8,9},{11,10... | collective-permute-start | bytes 18728 | tf_op jit(solution)/shard_map/ppermute | solution.py:18
  103.1 4.1 %copy-start.40 = (f32[258]{0:T(512)S(1)}, f32[258]{0:T(512)}, u32[]{:S(2)}) copy-start(f32[258]{0:T(512)} %fusion.61) | copy-start | bytes 3100
  117.7 6.7 %copy-start.4 = (f32[4,256,128]{2,0,1:T(4,128)}, f32[4,256,128]{2,0,1:T(4,128)S(1)}, u32[]{:S(2)}) copy-start(f32[4,256,128]{2,0,1:T(4,128)S(1)} %broadcast_divide_fusion.4) | copy-start | bytes 1572868
  119.0 11.7 %collective-permute-start.9 = (f32[4,256,1]{2,0,1:T(4,128)}, f32[4,256,1]{2,0,1:T(4,128)}, u32[]{:S(2)}, u32[]{:S(2)}) collective-permute-start(f32[4,256,1]{2,0,1:T(4,128)} %get-tuple-element.131), channel_id=1, source_target_pairs={{0,2},{2,4},{4,6},{6,8},{8,10},{10,12},{12,14},{14,16},{16,18},{18... | collective-permute-start | bytes 12296 | tf_op jit(solution)/shard_map/ppermute | solution.py:16
  119.0 12.9 %collective-permute-start.8 = (f32[4,256,1]{2,0,1:T(4,128)}, f32[4,256,1]{2,0,1:T(4,128)}, u32[]{:S(2)}, u32[]{:S(2)}) collective-permute-start(f32[4,256,1]{2,0,1:T(4,128)} %get-tuple-element.130), channel_id=1, source_target_pairs={{2,0},{4,2},{6,4},{8,6},{10,8},{12,10},{14,12},{16,14},{18,16},{20... | collective-permute-start | bytes 12296 | tf_op jit(solution)/shard_map/ppermute | solution.py:18
  124.5 12.2 %slice-start = ((f32[4,256,128]{2,0,1:T(4,128)}), f32[4,1,128]{2,0,1:T(4,128)S(1)}, s32[]{:S(2)}) async-start(f32[4,256,128]{2,0,1:T(4,128)} %copy-done.4), calls=%async_computation | async-start | bytes 4096 | tf_op jit(solution)/shard_map/slice | solution.py:78
  134.6 26.7 %collective-permute-start.10 = (f32[4,1,130]{1,0,2:T(4,128)S(1)}, f32[4,1,130]{1,0,2:T(4,128)}, u32[]{:S(2)}, u32[]{:S(2)}) collective-permute-start(f32[4,1,130]{1,0,2:T(4,128)S(1)} %get-tuple-element.116), channel_id=1, source_target_pairs={{1,0},{0,1},{3,2},{2,3},{5,4},{4,5},{7,6},{6,7},{9,8},{8,9},{11,10... | collective-permute-start | bytes 6248 | tf_op jit(solution)/shard_map/ppermute | solution.py:18
  136.4 24.9 %collective-permute-start.11 = (f32[4,1,130]{1,0,2:T(4,128)S(1)}, f32[4,1,130]{1,0,2:T(4,128)}, u32[]{:S(2)}, u32[]{:S(2)}) collective-permute-start(f32[4,1,130]{1,0,2:T(4,128)S(1)} %get-tuple-element.117), channel_id=1, source_target_pairs={{0,1},{1,0},{2,3},{3,2},{4,5},{5,4},{6,7},{7,6},{8,9},{9,8},{10,11... | collective-permute-start | bytes 6248 | tf_op jit(solution)/shard_map/ppermute | solution.py:16
  164.3 4.1 %copy-start.5 = (f32[4,256,128]{2,0,1:T(4,128)S(1)}, f32[4,256,128]{2,0,1:T(4,128)}, u32[]{:S(2)}) copy-start(f32[4,256,128]{2,0,1:T(4,128)} %copy-done.4) | copy-start | bytes 1572868
  171.5 6.7 %copy-start.6 = (f32[4,256,128]{2,0,1:T(4,128)}, f32[4,256,128]{2,0,1:T(4,128)S(1)}, u32[]{:S(2)}) copy-start(f32[4,256,128]{2,0,1:T(4,128)S(1)} %broadcast_divide_fusion.3) | copy-start | bytes 1572868
  172.8 11.7 %collective-permute-start.13 = (f32[4,256,1]{2,0,1:T(4,128)}, f32[4,256,1]{2,0,1:T(4,128)}, u32[]{:S(2)}, u32[]{:S(2)}) collective-permute-start(f32[4,256,1]{2,0,1:T(4,128)} %get-tuple-element.129), channel_id=1, source_target_pairs={{0,2},{2,4},{4,6},{6,8},{8,10},{10,12},{12,14},{14,16},{16,18},{18... | collective-permute-start | bytes 12296 | tf_op jit(solution)/shard_map/ppermute | solution.py:16
  173.1 12.6 %collective-permute-start.12 = (f32[4,256,1]{2,0,1:T(4,128)}, f32[4,256,1]{2,0,1:T(4,128)}, u32[]{:S(2)}, u32[]{:S(2)}) collective-permute-start(f32[4,256,1]{2,0,1:T(4,128)} %get-tuple-element.128), channel_id=1, source_target_pairs={{2,0},{4,2},{6,4},{8,6},{10,8},{12,10},{14,12},{16,14},{18,16},{20... | collective-permute-start | bytes 12296 | tf_op jit(solution)/shard_map/ppermute | solution.py:18
  178.2 12.2 %slice-start.1 = ((f32[4,256,128]{2,0,1:T(4,128)}), f32[4,1,128]{2,0,1:T(4,128)S(1)}, s32[]{:S(2)}) async-start(f32[4,256,128]{2,0,1:T(4,128)} %copy-done.6), calls=%async_computation.1 | async-start | bytes 4096 | tf_op jit(solution)/shard_map/slice | solution.py:78
  188.3 25.6 %collective-permute-start.14 = (f32[4,1,130]{1,0,2:T(4,128)S(1)}, f32[4,1,130]{1,0,2:T(4,128)}, u32[]{:S(2)}, u32[]{:S(2)}) collective-permute-start(f32[4,1,130]{1,0,2:T(4,128)S(1)} %get-tuple-element.112), channel_id=1, source_target_pairs={{1,0},{0,1},{3,2},{2,3},{5,4},{4,5},{7,6},{6,7},{9,8},{8,9},{11,10... | collective-permute-start | bytes 6248 | tf_op jit(solution)/shard_map/ppermute | solution.py:18
  190.0 23.9 %collective-permute-start.15 = (f32[4,1,130]{1,0,2:T(4,128)S(1)}, f32[4,1,130]{1,0,2:T(4,128)}, u32[]{:S(2)}, u32[]{:S(2)}) collective-permute-start(f32[4,1,130]{1,0,2:T(4,128)S(1)} %get-tuple-element.113), channel_id=1, source_target_pairs={{0,1},{1,0},{2,3},{3,2},{4,5},{5,4},{6,7},{7,6},{8,9},{9,8},{10,11... | collective-permute-start | bytes 6248 | tf_op jit(solution)/shard_map/ppermute | solution.py:16
  217.0 4.2 %copy-start.7 = (f32[4,256,128]{2,0,1:T(4,128)S(1)}, f32[4,256,128]{2,0,1:T(4,128)}, u32[]{:S(2)}) copy-start(f32[4,256,128]{2,0,1:T(4,128)} %copy-done.6) | copy-start | bytes 1572868
  221.1 2.5 copy-start.15
  226.4 11.7 %collective-permute-start.17 = (f32[4,256,1]{2,0,1:T(4,128)}, f32[4,256,1]{2,0,1:T(4,128)}, u32[]{:S(2)}, u32[]{:S(2)}) collective-permute-start(f32[4,256,1]{2,0,1:T(4,128)} %get-tuple-element.127), channel_id=1, source_target_pairs={{0,2},{2,4},{4,6},{6,8},{8,10},{10,12},{12,14},{14,16},{16,18},{18... | collective-permute-start | bytes 12296 | tf_op jit(solution)/shard_map/ppermute | solution.py:16
  226.7 12.6 %collective-permute-start.16 = (f32[4,256,1]{2,0,1:T(4,128)}, f32[4,256,1]{2,0,1:T(4,128)}, u32[]{:S(2)}, u32[]{:S(2)}) collective-permute-start(f32[4,256,1]{2,0,1:T(4,128)} %get-tuple-element.126), channel_id=1, source_target_pairs={{2,0},{4,2},{6,4},{8,6},{10,8},{12,10},{14,12},{16,14},{18,16},{20... | collective-permute-start | bytes 12296 | tf_op jit(solution)/shard_map/ppermute | solution.py:18
  240.6 3.0 copy-start.41
  241.6 30.1 %collective-permute-start.18 = (f32[4,1,130]{1,0,2:T(4,128)}, f32[4,1,130]{1,0,2:T(4,128)}, u32[]{:S(2)}, u32[]{:S(2)}) collective-permute-start(f32[4,1,130]{1,0,2:T(4,128)} %get-tuple-element.108), channel_id=1, source_target_pairs={{1,0},{0,1},{3,2},{2,3},{5,4},{4,5},{7,6},{6,7},{9,8},{8,9},{11,10... | collective-permute-start | bytes 6248 | tf_op jit(solution)/shard_map/ppermute | solution.py:18
  243.1 28.5 %collective-permute-start.19 = (f32[4,1,130]{1,0,2:T(4,128)S(1)}, f32[4,1,130]{1,0,2:T(4,128)}, u32[]{:S(2)}, u32[]{:S(2)}) collective-permute-start(f32[4,1,130]{1,0,2:T(4,128)S(1)} %get-tuple-element.109), channel_id=1, source_target_pairs={{0,1},{1,0},{2,3},{3,2},{4,5},{5,4},{6,7},{7,6},{8,9},{9,8},{10,11... | collective-permute-start | bytes 6248 | tf_op jit(solution)/shard_map/ppermute | solution.py:16
  283.3 11.7 %collective-permute-start.21 = (f32[4,256,1]{2,0,1:T(4,128)}, f32[4,256,1]{2,0,1:T(4,128)}, u32[]{:S(2)}, u32[]{:S(2)}) collective-permute-start(f32[4,256,1]{2,0,1:T(4,128)} %get-tuple-element.125), channel_id=1, source_target_pairs={{0,2},{2,4},{4,6},{6,8},{8,10},{10,12},{12,14},{14,16},{16,18},{18... | collective-permute-start | bytes 12296 | tf_op jit(solution)/shard_map/ppermute | solution.py:16
  283.6 12.6 %collective-permute-start.20 = (f32[4,256,1]{2,0,1:T(4,128)}, f32[4,256,1]{2,0,1:T(4,128)}, u32[]{:S(2)}, u32[]{:S(2)}) collective-permute-start(f32[4,256,1]{2,0,1:T(4,128)} %get-tuple-element.124), channel_id=1, source_target_pairs={{2,0},{4,2},{6,4},{8,6},{10,8},{12,10},{14,12},{16,14},{18,16},{20... | collective-permute-start | bytes 12296 | tf_op jit(solution)/shard_map/ppermute | solution.py:18
  297.4 3.0 copy-start.42
  298.4 29.8 %collective-permute-start.22 = (f32[4,1,130]{1,0,2:T(4,128)}, f32[4,1,130]{1,0,2:T(4,128)}, u32[]{:S(2)}, u32[]{:S(2)}) collective-permute-start(f32[4,1,130]{1,0,2:T(4,128)} %get-tuple-element.104), channel_id=1, source_target_pairs={{1,0},{0,1},{3,2},{2,3},{5,4},{4,5},{7,6},{6,7},{9,8},{8,9},{11,10... | collective-permute-start | bytes 6248 | tf_op jit(solution)/shard_map/ppermute | solution.py:18
  300.0 28.2 %collective-permute-start.23 = (f32[4,1,130]{1,0,2:T(4,128)S(1)}, f32[4,1,130]{1,0,2:T(4,128)}, u32[]{:S(2)}, u32[]{:S(2)}) collective-permute-start(f32[4,1,130]{1,0,2:T(4,128)S(1)} %get-tuple-element.105), channel_id=1, source_target_pairs={{0,1},{1,0},{2,3},{3,2},{4,5},{5,4},{6,7},{7,6},{8,9},{9,8},{10,11... | collective-permute-start | bytes 6248 | tf_op jit(solution)/shard_map/ppermute | solution.py:16
  339.9 11.7 %collective-permute-start.25 = (f32[4,256,1]{2,0,1:T(4,128)}, f32[4,256,1]{2,0,1:T(4,128)}, u32[]{:S(2)}, u32[]{:S(2)}) collective-permute-start(f32[4,256,1]{2,0,1:T(4,128)} %get-tuple-element.123), channel_id=1, source_target_pairs={{0,2},{2,4},{4,6},{6,8},{8,10},{10,12},{12,14},{14,16},{16,18},{18... | collective-permute-start | bytes 12296 | tf_op jit(solution)/shard_map/ppermute | solution.py:16
  340.2 12.6 %collective-permute-start.24 = (f32[4,256,1]{2,0,1:T(4,128)}, f32[4,256,1]{2,0,1:T(4,128)}, u32[]{:S(2)}, u32[]{:S(2)}) collective-permute-start(f32[4,256,1]{2,0,1:T(4,128)} %get-tuple-element.122), channel_id=1, source_target_pairs={{2,0},{4,2},{6,4},{8,6},{10,8},{12,10},{14,12},{16,14},{18,16},{20... | collective-permute-start | bytes 12296 | tf_op jit(solution)/shard_map/ppermute | solution.py:18
  355.1 25.6 %collective-permute-start.26 = (f32[4,1,130]{1,0,2:T(4,128)}, f32[4,1,130]{1,0,2:T(4,128)}, u32[]{:S(2)}, u32[]{:S(2)}) collective-permute-start(f32[4,1,130]{1,0,2:T(4,128)} %get-tuple-element.100), channel_id=1, source_target_pairs={{1,0},{0,1},{3,2},{2,3},{5,4},{4,5},{7,6},{6,7},{9,8},{8,9},{11,10... | collective-permute-start | bytes 6248 | tf_op jit(solution)/shard_map/ppermute | solution.py:18
  356.6 24.1 %collective-permute-start.27 = (f32[4,1,130]{1,0,2:T(4,128)S(1)}, f32[4,1,130]{1,0,2:T(4,128)}, u32[]{:S(2)}, u32[]{:S(2)}) collective-permute-start(f32[4,1,130]{1,0,2:T(4,128)S(1)} %get-tuple-element.101), channel_id=1, source_target_pairs={{0,1},{1,0},{2,3},{3,2},{4,5},{5,4},{6,7},{7,6},{8,9},{9,8},{10,11... | collective-permute-start | bytes 6248 | tf_op jit(solution)/shard_map/ppermute | solution.py:16
  (29 other events, 54.3 us)
where the time goes:
time: 393 us; the launch traced here: 390 us
  blocking collectives  163 us (41%)
  local copies, waits for them, and re-layouts  90.6 us (23%)
  other arithmetic  49.4 us (13%)
  starting transfers between devices  46.6 us (12%)
  waiting for transfers between devices  40.4 us (10%)
    all_gather x6, blocking collectives, fold_mirror(): whole_row = lax.all_gather(top_row, 'lon', axis=1, tiled=True)  123 us
    ppermute x14, starting transfers between devices, with_halo(): lax.ppermute(head, axis, [((i + 1) % count, i) for i in range(count)])  40.5 us
    ppermute x14, waiting for transfers between devices, with_halo(): lax.ppermute(tail, axis, [(i, (i + 1) % count) for i in range(count)])  38 us
    unnamed x106, local copies, waits for them, and re-layouts  27 us
    all_gather x1, blocking collectives, per_device(): lax.all_gather(top_y, 'lon', axis=1, tiled=True)  21.7 us
    concatenate x12, other arithmetic, with_halo(): jnp.concatenate([lax.ppermute(tail, axis, [(i, (i + 1) % count) for i in...  19.9 us
    all_gather x1, blocking collectives, per_device(): lax.all_gather(top_sea, 'lon', axis=1, tiled=True)  17.8 us
    gather x12, local copies, waits for them, and re-layouts, fold_mirror(): return jnp.take(whole_row, targets, axis=1)  15.4 us
  transfers between devices with their start and end apart: 28, of which 7 were waited for; matrix products, arithmetic and copies ran while one was open for 13% of the time, Pallas kernels for 0%

commit v1 on v0

v1 whole, which is shorter than its diff:
```python
import functools

import jax
import jax.numpy as jnp
from jax import lax
from jax.experimental import pallas as pl
from jax.experimental.pallas import tpu as pltpu
from jax.sharding import PartitionSpec as P

STEPS = 6
LEV = 4
LANES = 128
SUB = 8
PAIR = LANES // 2
EDGES = LEV // 2
WEST = STEPS
EAST = 4 * STEPS
OWN = 2 * STEPS
PART = 4 * STEPS * EDGES
PLANES = 3 * LEV + 1
ALL = PLANES + 3 * EDGES + 1
VMEM_LIMIT = 60 * 1024 * 1024
F32 = jnp.float32


def lanes_of(shape):
    return lax.broadcasted_iota(jnp.int32, shape, 1)


def roll(x, shift):
    shift = shift % LANES
    return x if shift == 0 else pltpu.roll(x, shift, 1)


def half_lane(shape):
    return jnp.bitwise_and(lanes_of(shape), PAIR - 1)


def pair_up(low, high, shape):
    return jnp.where(lanes_of(shape) < PAIR, low, high)


def own_ends(low, high):
    shape = low.shape
    at = half_lane(shape)
    west = pair_up(roll(low, WEST), roll(high, PAIR + WEST), shape)
    east = pair_up(roll(low, EAST + OWN), roll(high, PAIR + EAST + OWN), shape)
    out = jnp.where((at >= WEST) & (at < WEST + OWN), west, 0.0)
    return jnp.where((at >= EAST) & (at < EAST + OWN), east, out)


def raw_fields(l, rows, inc, kx, ky, mx, my, mask, r):
    sea = mask[l, rows, :].astype(F32)
    return inc[l, rows, :] * r, kx[l, rows, :] * mx * sea, ky[l, rows, :] * my * sea


def pack_kernel(par, inc, kx, ky, mx, my, area, mask, edge_ref, m0_ref, m1_ref, acc0, acc1):
    half = inc.shape[1]
    chunk = 32
    even = par[0] == 0
    is_first = pl.program_id(0) == 0
    lane = lanes_of((chunk, LANES))
    for row in range(0, half, chunk):
        rows = pl.ds(row, chunk)
        r = 1.0 / area[rows, :]
        mxv, myv = mx[rows, :], my[rows, :]
        first = jnp.zeros((chunk, LANES), F32)
        last = jnp.zeros((chunk, LANES), F32)
        for l in range(LEV):
            fields = raw_fields(l, rows, inc, kx, ky, mxv, myv, mask, r) + (r,)
            for p, plane in enumerate(fields):
                at = PAIR * (l % 2) + 4 * STEPS * (l // 2) + STEPS * p
                here = (lane >= at) & (lane < at + STEPS)
                first = jnp.where(here, roll(plane, at), first)
                last = jnp.where(here, roll(plane, at + STEPS), last)
            store_edge(is_first, row, half, [(p * LEV + l, f) for p, f in enumerate(fields[:3])], edge_ref)
        store_edge(is_first, row, half, [(3 * LEV, r)], edge_ref)
        acc0[rows, :] = jnp.where(even, last, first)
        acc1[rows, :] = jnp.where(even, first, last)
    for acc, ref in ((acc0, m0_ref), (acc1, m1_ref)):
        turned = jnp.transpose(acc[...])
        ref[pl.ds(0, PART), :] = turned[:PART]
        ref[pl.ds(PART, PART), :] = turned[PAIR : PAIR + PART]


def store_edge(is_first, row, half, planes, edge_ref):
    side = 2 * SUB
    if row == 0:

        @pl.when(is_first)
        def _():
            for plane, value in planes:
                edge_ref[plane] = value[:side]

    if row == half - 2 * side:

        @pl.when(jnp.logical_not(is_first))
        def _():
            for plane, value in planes:
                edge_ref[plane] = value[side:]


def pack(par, inc, kx, ky, mx, my, area, mask):
    half = inc.shape[1] // 2
    cube = pl.BlockSpec((LEV, half, LANES), lambda i: (0, i, 0))
    flat = pl.BlockSpec((half, LANES), lambda i: (i, 0))
    msg = pl.BlockSpec((2 * PART, LANES), lambda i: (i, 0))
    msg_out = jax.ShapeDtypeStruct((4 * PART, LANES), F32)
    return pl.pallas_call(
        pack_kernel,
        grid=(2,),
        in_specs=[pl.BlockSpec(memory_space=pltpu.SMEM), cube, cube, cube, flat, flat, flat, cube],
        out_specs=[pl.BlockSpec((PLANES, 2 * SUB, LANES), lambda i: (0, 1 - i, 0)), msg, msg],
        out_shape=[jax.ShapeDtypeStruct((PLANES, 4 * SUB, LANES), F32), msg_out, msg_out],
        scratch_shapes=[pltpu.VMEM((half, LANES), F32), pltpu.VMEM((half, LANES), F32)],
        compiler_params=pltpu.CompilerParams(vmem_limit_bytes=VMEM_LIMIT),
        name="pack",
    )(par, inc, kx, ky, mx, my, area, mask)


def untranspose(msg_ref, half, buf):
    buf[pl.ds(0, PART), :] = msg_ref[pl.ds(2 * PART * half, PART), :]
    buf[pl.ds(PAIR, PART), :] = msg_ref[pl.ds(2 * PART * half + PART, PART), :]
    return jnp.transpose(buf[...])


def halo_half(par, g0, g1, half, buf):
    t0 = untranspose(g0, half, buf)
    t1 = untranspose(g1, half, buf)
    even = par[0] == 0
    return jnp.where(even, t1, t0), jnp.where(even, t0, t1)


def with_halo(own, west_t, east_t, e, p):
    at = half_lane(own.shape)
    slot = 4 * STEPS * e + STEPS * p
    out = jnp.where(at < WEST, roll(west_t, -slot), own)
    return jnp.where((at >= EAST + OWN) & (at < EAST + OWN + STEPS), roll(east_t, EAST + OWN - slot), out)


def edge_kernel(par, g0, g1, edge, hedge_ref, a_ref, b_ref, buf):
    rows = edge.shape[1]
    side = rows // 2
    lat_even = par[1] == 0
    buf[...] = jnp.zeros_like(buf)
    turned = []
    for half, lo in ((1, LANES - side), (0, 0)):
        wt, et = halo_half(par, g0, g1, half, buf)
        turned.append((wt[lo : lo + side], et[lo : lo + side]))
    west_t, east_t = [jnp.concatenate([turned[0][i], turned[1][i]], axis=0) for i in range(2)]
    for k in range(3 * EDGES + 1):
        p, e = divmod(k, EDGES)
        low, high = (edge[p * LEV + 2 * e], edge[p * LEV + 2 * e + 1]) if p < 3 else (edge[3 * LEV],) * 2
        value = with_halo(own_ends(low, high), west_t, east_t, e, p)
        hedge_ref[k] = value
        last, first = value[side - SUB : side], value[side : side + SUB]
        a_ref[PLANES + k] = jnp.where(lat_even, last, first)
        b_ref[PLANES + k] = jnp.where(lat_even, first, last)
    for p in range(PLANES):
        last, first = edge[p, side - SUB : side, :], edge[p, side : side + SUB, :]
        a_ref[p] = jnp.where(lat_even, last, first)
        b_ref[p] = jnp.where(lat_even, first, last)


def edge_messages(par, g0, g1, edge):
    vm = pl.BlockSpec(memory_space=pltpu.VMEM)
    msg = jax.ShapeDtypeStruct((ALL, SUB, LANES), F32)
    return pl.pallas_call(
        edge_kernel,
        in_specs=[pl.BlockSpec(memory_space=pltpu.SMEM), vm, vm, vm],
        out_specs=[vm, vm, vm],
        out_shape=[jax.ShapeDtypeStruct((ALL - PLANES, edge.shape[1], LANES), F32), msg, msg],
        scratch_shapes=[pltpu.VMEM((LANES, LANES), F32)],
        compiler_params=pltpu.CompilerParams(vmem_limit_bytes=VMEM_LIMIT),
        name="edge",
    )(par, g0, g1, edge)


def coefficients(x, y, r, c, at, n, coef, weights=None):
    rows, up, down = pl.ds(at, n), pl.ds(at + 1, n), pl.ds(at - 1, n)
    here = x[c, rows, :]
    xe, xw = roll(here, -1), roll(here, 1)
    sea = jnp.where(here > 0, 1.0, 0.0)
    yv, ys = y[c, rows, :], y[c, down, :]
    east = jnp.where(xe > 0, here, 0.0)
    west = xw * sea
    north = jnp.where(x[c, up, :] > 0, yv, 0.0)
    south = ys * sea
    if weights is not None:
        flip, n_own, n_far, s_own, s_far = weights
        sea_s = jnp.where(x[c, down, :] > 0, 1.0, 0.0)
        east = jnp.where(flip, xe * sea, east)
        west = jnp.where(flip, jnp.where(xw > 0, here, 0.0), west)
        north = n_own * north + n_far * (y[c, up, :] * sea)
        south = s_own * south + s_far * (yv * sea_s)
    east, west, north, south = r * east, r * west, r * north, r * south
    coef[0, c, rows, :] = east
    coef[1, c, rows, :] = west
    coef[2, c, rows, :] = north
    coef[3, c, rows, :] = south
    coef[4, c, rows, :] = 1.0 - ((east + west) + (north + south))


def advance(src, dst, coef, c, at, n):
    rows = pl.ds(at, n)
    here = src[c, rows, :]
    lon = coef[0, c, rows, :] * roll(here, -1) + coef[1, c, rows, :] * roll(here, 1)
    lat = coef[2, c, rows, :] * src[c, pl.ds(at + 1, n), :] + coef[3, c, rows, :] * src[c, pl.ds(at - 1, n), :]
    dst[c, rows, :] = coef[4, c, rows, :] * here + (lon + lat)


def run_steps(one, two, coef, count, lo, hi, n):
    def both(_, carry):
        for src, dst in ((one, two), (two, one)):
            for at in range(lo, hi, n):
                for c in range(count):
                    advance(src, dst, coef, c, at, n)
        return carry

    lax.fori_loop(0, STEPS // 2, both, 0)


def clear_pads(refs, count, lo, hi):
    zero = jnp.zeros((SUB, LANES), F32)
    for ref in refs:
        for c in range(count):
            ref[c, pl.ds(lo - SUB, SUB), :] = zero
            ref[c, pl.ds(hi, SUB), :] = zero


def inner_kernel(inc, kx, ky, mx, my, area, mask, out_ref, ends_ref, one, two, xb, yb, coef, kept):
    rows = inc.shape[1]
    n = 64
    lo, hi = SUB, SUB + rows
    odd = lax.rem(pl.program_id(0), 2) == 1
    clear_pads((one, two, xb, yb), 1, lo, hi)
    for at in range(0, rows, n):
        here, there = pl.ds(at, n), pl.ds(lo + at, n)
        r = 1.0 / area[here, :]
        w, rx, ry = raw_fields(0, here, inc, kx, ky, mx[here, :], my[here, :], mask, r)
        one[0, there, :] = w
        xb[0, there, :] = rx
        yb[0, there, :] = ry
        for k, value in enumerate((w, rx, ry, r)):

            @pl.when(jnp.logical_not(odd))
            def _():
                kept[k, here, :] = value

            @pl.when(odd)
            def _():
                ends_ref[0, k, here, :] = own_ends(kept[k, here, :], value)

    for at in range(lo, hi, n):
        coefficients(xb, yb, 1.0 / area[pl.ds(at - lo, n), :], 0, at, n, coef)
    run_steps(one, two, coef, 1, lo, hi, n)
    out_ref[0] = one[0, pl.ds(lo, rows), :]


def inner(inc, kx, ky, mx, my, area, mask):
    rows = inc.shape[1]
    cube = pl.BlockSpec((1, rows, LANES), lambda i: (i, 0, 0))
    flat = pl.BlockSpec((rows, LANES), lambda i: (0, 0))
    pad = rows + 2 * SUB
    cells = pltpu.VMEM((1, pad, LANES), F32)
    return pl.pallas_call(
        inner_kernel,
        grid=(LEV,),
        in_specs=[cube, cube, cube, flat, flat, flat, cube],
        out_specs=[cube, pl.BlockSpec((1, 4, rows, LANES), lambda i: (i // 2, 0, 0, 0))],
        out_shape=[jax.ShapeDtypeStruct(inc.shape, F32), jax.ShapeDtypeStruct((EDGES, 4, rows, LANES), F32)],
        scratch_shapes=[
            cells,
            cells,
            cells,
            cells,
            pltpu.VMEM((5, 1, pad, LANES), F32),
            pltpu.VMEM((4, rows, LANES), F32),
        ],
        compiler_params=pltpu.CompilerParams(vmem_limit_bytes=VMEM_LIMIT),
        cost_estimate=pl.CostEstimate(flops=12_000_000, bytes_accessed=6_000_000, transcendentals=0),
        name="inner",
    )(inc, kx, ky, mx, my, area, mask)


def merge(own, ends, l):
    lane = lanes_of(own.shape)
    at = PAIR * (l % 2)
    out = jnp.where(lane < STEPS, roll(ends, -(at + WEST)), own)
    return jnp.where(lane >= LANES - STEPS, roll(ends, -(at + EAST + OWN)), out)


def ends_kernel(par, ends, g0, g1, mid, norm, area, out_ref, scale_ref, one, two, xb, yb, rb, coef, buf):
    rows = mid.shape[1]
    n = 64
    lo, hi = SUB, SUB + rows
    buf[...] = jnp.zeros_like(buf)
    clear_pads((one, two, xb, yb), EDGES, lo, hi)
    for half in range(2):
        wt, et = halo_half(par, g0, g1, half, buf)
        here, there = pl.ds(half * LANES, LANES), pl.ds(lo + half * LANES, LANES)
        for e in range(EDGES):
            one[e, there, :] = with_halo(ends[e, 0, here, :], wt, et, e, 0)
            xb[e, there, :] = with_halo(ends[e, 1, here, :], wt, et, e, 1)
            yb[e, there, :] = with_halo(ends[e, 2, here, :], wt, et, e, 2)
        rb[there, :] = with_halo(ends[0, 3, here, :], wt, et, 0, 3)
    for at in range(lo, hi, n):
        for e in range(EDGES):
            coefficients(xb, yb, rb[pl.ds(at, n), :], e, at, n, coef)
    run_steps(one, two, coef, EDGES, lo, hi, n)
    for l in range(LEV):
        scale = norm[l] * area[...]
        out_ref[l] = scale * merge(mid[l], one[l // 2, pl.ds(lo, rows), :], l)
        scale_ref[l, :SUB, :] = scale[rows - SUB :]
        scale_ref[l, SUB:, :] = scale[:SUB]


def lon_ends(par, ends, g0, g1, mid, norm, area):
    rows = mid.shape[1]
    vm = pl.BlockSpec(memory_space=pltpu.VMEM)
    pad = rows + 2 * SUB
    cells = pltpu.VMEM((EDGES, pad, LANES), F32)
    return pl.pallas_call(
        ends_kernel,
        in_specs=[pl.BlockSpec(memory_space=pltpu.SMEM)] + [vm] * 6,
        out_specs=[vm, vm],
        out_shape=[jax.ShapeDtypeStruct(mid.shape, F32), jax.ShapeDtypeStruct((LEV, 2 * SUB, LANES), F32)],
        scratch_shapes=[
            cells,
            cells,
            cells,
            cells,
            pltpu.VMEM((pad, LANES), F32),
            pltpu.VMEM((5, EDGES, pad, LANES), F32),
            pltpu.VMEM((LANES, LANES), F32),
        ],
        compiler_params=pltpu.CompilerParams(vmem_limit_bytes=VMEM_LIMIT),
        cost_estimate=pl.CostEstimate(flops=8_000_000, bytes_accessed=4_000_000, transcendentals=0),
        name="ends",
    )(par, ends, g0, g1, mid, norm, area)


def gather(x, idx):
    return jnp.take_along_axis(x, idx, axis=1)


def mirrored(b1, b2, first):
    shape = (SUB, LANES)
    lane, at = lanes_of(shape), half_lane(shape)
    flip = SUB - 1 - lax.broadcasted_iota(jnp.int32, shape, 0)
    own_j = first - lane
    own_i = jnp.bitwise_and(own_j, LANES - 1)
    end_j = first - jnp.where(at < EAST, at - WEST, at - EAST + LANES - OWN)
    end_i = jnp.bitwise_and(end_j, LANES - 1)

    def rows(x):
        return jnp.take_along_axis(x, flip, axis=0)

    def pick(j, idx, beyond1, one, two, beyond2):
        out = jnp.where(j >= 0, gather(one, idx), gather(two, idx))
        out = jnp.where(j >= LANES, gather(beyond1, idx), out)
        return jnp.where(j < -LANES, gather(beyond2, idx), out)

    out = {}
    for k in range(3 * EDGES + 1):
        p, e = divmod(k, EDGES)
        ends1, ends2 = b1[PLANES + k], b2[PLANES + k]
        both = []
        for q in range(2):
            plane = p * LEV + 2 * e + q if p < 3 else 3 * LEV
            one, two = b1[plane], b2[plane]
            if p < 3 or q == 0:
                out[plane] = rows(jnp.where(own_j >= 0, gather(one, own_i), gather(two, own_i)))
            beyond1 = roll(ends1, -(PAIR * q + EAST + OWN))
            beyond2 = roll(ends2, -(PAIR * q + WEST))
            both.append(pick(end_j, end_i, beyond1, one, two, beyond2))
        out[PLANES + k] = rows(pair_up(both[0], both[1], shape))
    return out


def band_kernel(par, edge, hedge, ga, gb, gc, scale, old, out_ref, one, two, xb, yb, rb, coef, res, sem):
    del old
    side = edge.shape[1] // 2
    count = LEV + EDGES
    lat_even = par[1] == 0
    is_top = par[2] == 1
    lo = SUB
    north, south, own = lo + side, lo + side + SUB, lo + side + 2 * SUB
    hi = own + side
    clear_pads((one, two, xb, yb), count, lo, hi)

    def place(plane):
        if plane < 3 * LEV:
            return (one, xb, yb)[plane // LEV].at[plane % LEV]
        if plane == 3 * LEV:
            return rb.at[0]
        p, e = divmod(plane - PLANES, EDGES)
        return rb.at[1] if p == 3 else (one, xb, yb)[p].at[LEV + e]

    for plane in range(ALL):
        ref = place(plane)
        mine = edge.at[plane] if plane < PLANES else hedge.at[plane - PLANES]
        ref[pl.ds(lo, side), :] = mine[:side, :]
        ref[pl.ds(own, side), :] = mine[side:, :]
        ref[pl.ds(south, SUB), :] = jnp.where(lat_even, gb[plane], ga[plane])

    @pl.when(is_top)
    def _():
        for plane, value in mirrored(gb, gc, par[3]).items():
            place(plane)[pl.ds(north, SUB), :] = value

    @pl.when(jnp.logical_not(is_top))
    def _():
        for plane in range(ALL):
            place(plane)[pl.ds(north, SUB), :] = jnp.where(lat_even, ga[plane], gb[plane])

    n = hi - lo
    row = lo + lax.broadcasted_iota(jnp.int32, (n, LANES), 0)
    fold = is_top & (row >= north) & (row < south)
    n_far = jnp.where(is_top & (row == north - 1), 0.5, jnp.where(fold, 1.0, 0.0))
    s_far = jnp.where(is_top & (row == north), 0.5, jnp.where(fold, 1.0, 0.0))
    weights = (fold, 1.0 - n_far, n_far, 1.0 - s_far, s_far)
    for c in range(count):
        coefficients(xb, yb, rb[c // LEV, pl.ds(lo, n), :], c, lo, n, coef, weights)
    run_steps(one, two, coef, count, lo, hi, n)
    for l in range(LEV):
        for i, at in enumerate((north - SUB, own)):
            rows = pl.ds(at, SUB)
            value = merge(one[l, rows, :], one[LEV + l // 2, rows, :], l)
            res[i, l] = scale[l, i * SUB : (i + 1) * SUB, :] * value
    rows = out_ref.shape[1]
    copies = [
        pltpu.make_async_copy(res.at[0], out_ref.at[:, pl.ds(rows - SUB, SUB), :], sem.at[0]),
        pltpu.make_async_copy(res.at[1], out_ref.at[:, pl.ds(0, SUB), :], sem.at[1]),
    ]
    for copy in copies:
        copy.start()
    for copy in copies:
        copy.wait()


def band(par, edge, hedge, ga, gb, gc, scale, out):
    vm = pl.BlockSpec(memory_space=pltpu.VMEM)
    anywhere = pl.BlockSpec(memory_space=pl.ANY)
    pad = edge.shape[1] + 4 * SUB
    cells = pltpu.VMEM((LEV + EDGES, pad, LANES), F32)
    return pl.pallas_call(
        band_kernel,
        in_specs=[pl.BlockSpec(memory_space=pltpu.SMEM)] + [vm] * 6 + [anywhere],
        out_specs=anywhere,
        out_shape=jax.ShapeDtypeStruct(out.shape, F32),
        input_output_aliases={7: 0},
        scratch_shapes=[
            cells,
            cells,
            cells,
            cells,
            pltpu.VMEM((2, pad, LANES), F32),
            pltpu.VMEM((5, LEV + EDGES, pad, LANES), F32),
            pltpu.VMEM((2, LEV, SUB, LANES), F32),
            pltpu.SemaphoreType.DMA((2,)),
        ],
        compiler_params=pltpu.CompilerParams(vmem_limit_bytes=VMEM_LIMIT),
        name="band",
    )(par, edge, hedge, ga, gb, gc, scale, out)


def table(axes, sizes, send):
    place = {axis: i for i, axis in enumerate(axes)}

    def flat(lon, lat):
        spot = {"lon": lon, "lat": lat}
        index = 0
        for axis in axes:
            index = index * sizes[axis] + spot[axis]
        return index

    pairs = []
    for lon in range(sizes["lon"]):
        for lat in range(sizes["lat"]):
            to = send(lon, lat)
            if to is not None:
                pairs.append((flat(lon, lat), flat(to[0] % sizes["lon"], to[1])))
    return pairs


def per_device(axes, sizes, inc, kx, ky, mx, my, area, mask, fold_partner, norm):
    n_lon, n_lat = sizes["lon"], sizes["lat"]
    cols = inc.shape[2]
    lon, lat = lax.axis_index("lon"), lax.axis_index("lat")
    center = lax.rem(fold_partner[0] + lon * cols, n_lon * cols)
    fold_block = center // cols
    par = jnp.stack(
        [lax.rem(lon, 2), lax.rem(lat, 2), jnp.where(lat == n_lat - 1, 1, 0), lax.rem(center, cols)]
    ).astype(jnp.int32)

    def permute(x, send):
        return lax.ppermute(x, axes, table(axes, sizes, send))

    edge, m0, m1 = pack(par, inc, kx, ky, mx, my, area, mask)
    g0 = permute(m0, lambda o, a: (o + 1 - 2 * (o % 2), a))
    g1 = permute(m1, lambda o, a: (o - 1 + 2 * (o % 2), a))
    mid, ends = inner(inc, kx, ky, mx, my, area, mask)
    hedge, ma, mb = edge_messages(par, g0, g1, edge)
    ga = permute(ma, lambda o, a: (o, a + 1 - 2 * (a % 2)))

    def fold_exchange(block):
        def first(o, a):
            if a == n_lat - 1:
                return block - o, a
            to = a - 1 + 2 * (a % 2)
            return (o, to) if 0 <= to < n_lat else None

        def second(o, a):
            return (block - 1 - o, a) if a == n_lat - 1 else None

        def exchange(x, *others):
            return (permute(x, first), permute(x, second)) + tuple(lon_ends(par, *others))

        return exchange

    branches = [fold_exchange(block) for block in range(n_lon)]
    gb, gc, out, scale = lax.switch(fold_block, branches, mb, ends, g0, g1, mid, norm, area)
    return band(par, edge, hedge, ga, gb, gc, scale, out)


def solution(mesh):
    axes = tuple(mesh.axis_names)
    sizes = dict(mesh.shape)
    cube, flat = P(None, "lat", "lon"), P("lat", "lon")
    return jax.shard_map(
        functools.partial(per_device, axes, sizes),
        mesh=mesh,
        in_specs=(cube, cube, cube, flat, flat, flat, cube, P("lon"), cube),
        out_specs=cube,
        check_vma=False,
    )
```

time: 393 us -> 39.5 us (0.10)
  the two profiles are of different devices: /device:TPU:0 before, /device:TPU:4 now
where the time goes in v1:
time: 39.5 us; the launch traced here: 38.9 us
  Pallas kernels  21.2 us (54%)
  starting transfers between devices  13.4 us (34%)
  waiting for transfers between devices  2.54 us (6%)
  local copies, waits for them, and re-layouts  1.28 us (3%)
    ppermute x5, starting transfers between devices, permute(): return lax.ppermute(x, axes, table(axes, sizes, send))  13.4 us
    pallas_call x1, Pallas kernels, inner(): pl.pallas_call(inner_kernel, grid=(LEV,), in_specs=[cube, cube, cube, fla...  8.38 us
    pallas_call x1, Pallas kernels, pack(): pl.pallas_call(pack_kernel, grid=(2,), in_specs=[pl.BlockSpec(memory_spac...  4.34 us
    pallas_call x1, Pallas kernels, lon_ends(): pl.pallas_call(ends_kernel, in_specs=[pl.BlockSpec(memory_space=pltpu.SME...  3.42 us
    pallas_call x1, Pallas kernels, band(): pl.pallas_call(band_kernel, in_specs=[pl.BlockSpec(memory_space=pltpu.SME...  3.12 us
    ppermute x5, waiting for transfers between devices, permute(): return lax.ppermute(x, axes, table(axes, sizes, send))  2.54 us
    pallas_call x1, Pallas kernels, edge_messages(): pl.pallas_call(edge_kernel, in_specs=[pl.BlockSpec(memory_space=pltpu.SME...  1.98 us
    unnamed x8, local copies, waits for them, and re-layouts  1.28 us
  transfers between devices with their start and end apart: 5, of which 1 were waited for; matrix products, arithmetic and copies ran while one was open for 0% of the time, Pallas kernels for 30%

profile of v1, /device:TPU:4, one launch (start us, length us, event | category | flops | bytes accessed | tf_op | source)
XLA Modules:
  0.0 38.9 jit_solution(7867899472226958808)
XLA Ops:
  0.0 0.0 copy-start.3
  0.0 0.7 %copy-done.3 = s32[128]{0:T(128)S(1)} copy-done((s32[128]{0:T(128)S(1)}, s32[128]{0:T(128)}, u32[]{:S(2)}) %copy-start.3) | copy-done | bytes 536
  0.7 0.1 pad_add_fusion.par
  0.8 4.3 %pack.1 = (f32[13,32,128]{2,1,0:T(8,128)}, f32[192,128]{1,0:T(8,128)}, f32[192,128]{1,0:T(8,128)}) custom-call(s32[4]{0:T(128)S(1)} %pad_add_fusion.par, f32[4,256,128]{2,1,0:T(8,128)} %inc.3, f32[4,256,128]{2,1,0:T(8,128)} %kx.3, f32[4,256,128]{2,1,0:T(8,128)} %ky.3, f32[256,128]{1,0:T(8,128)} %mx.3, f32[256,128]{1,0:T(8,128)} %my.3, f32[256,128]{1,0:T(8,128)} %area.3, ...), custom_call_target="tpu_custom_call" | custom-call | tf_op jit(solution)/shard_map/pack/pallas_call | solution.py:109
  5.1 0.1 collective-permute-start.32
  5.2 4.6 %collective-permute-start.33 = (f32[192,128]{1,0:T(8,128)}, f32[192,128]{1,0:T(8,128)S(1)}, u32[]{:S(2)}, u32[]{:S(2)}) collective-permute-start(f32[192,128]{1,0:T(8,128)} %get-tuple-element.435), channel_id=1, source_target_pairs={{0,30},{1,31},{2,4},{3,5},{4,2},{5,3},{6,8},{7,9},{8,6},{9,7},{10,... | collective-permute-start | bytes 294920 | tf_op jit(solution)/shard_map/ppermute | solution.py:498
  9.8 0.0 collective-permute-done.32.g0
  9.8 2.5 %collective-permute-done.33.g1 = f32[192,128]{1,0:T(8,128)S(1)} collective-permute-done((f32[192,128]{1,0:T(8,128)}, f32[192,128]{1,0:T(8,128)S(1)}, u32[]{:S(2)}, u32[]{:S(2)}) %collective-permute-start.33) | collective-permute-done | bytes 98336 | tf_op jit(solution)/shard_map/ppermute | solution.py:498
  12.4 0.0 copy-start.1
  12.4 2.0 %edge.1 = (f32[7,32,128]{2,1,0:T(8,128)}, f32[20,8,128]{2,1,0:T(8,128)}, f32[20,8,128]{2,1,0:T(8,128)S(1)}) custom-call(s32[4]{0:T(128)S(1)} %pad_add_fusion.par, f32[192,128]{1,0:T(8,128)S(1)} %collective-permute-done.32.g0, f32[192,128]{1,0:T(8,128)S(1)} %collective-permute-done.33.g1, f32[13,32,128]{2,1,0:T(8,128)} %get-tuple-element.433.edge), custom_call_target="tpu_custom_call" | custom-call | tf_op jit(solution)/shard_map/edge/pallas_call | solution.py:168
  14.4 0.5 %collective-permute-start.34 = (f32[20,8,128]{2,1,0:T(8,128)}, f32[20,8,128]{2,1,0:T(8,128)S(1)}, u32[]{:S(2)}, u32[]{:S(2)}) collective-permute-start(f32[20,8,128]{2,1,0:T(8,128)} %get-tuple-element.437), channel_id=1, source_target_pairs={{0,1},{1,0},{2,3},{3,2},{4,5},{5,4},{6,7},{7,6},{8,9},{9,8},{10,11... | collective-permute-start | bytes 245768 | tf_op jit(solution)/shard_map/ppermute | solution.py:498
  14.9 0.0 copy-done.1
  14.9 0.0 copy-start
  14.9 8.4 %inner.1 = (f32[4,256,128]{2,1,0:T(8,128)S(1)}, f32[2,4,256,128]{3,2,1,0:T(8,128)S(1)}) custom-call(f32[4,256,128]{2,1,0:T(8,128)} %inc.3, f32[4,256,128]{2,1,0:T(8,128)} %kx.3, f32[4,256,128]{2,1,0:T(8,128)} %ky.3, f32[256,128]{1,0:T(8,128)} %mx.3, f32[256,128]{1,0:T(8,128)} %my.3, f32[256,128]{1,0:T(8,128)S(1)} %copy-done.1, s32[4,256,128]{2,1,0:T(8,128)} %mask.3), custom_call_target="tpu_custom_call" | custom-call | flops 12000000 | bytes 6000000 | tf_op jit(solution)/shard_map/inner/pallas_call | solution.py:266
  23.3 0.0 copy-done
  23.3 11.7 %conditional.1 = (f32[20,8,128]{2,1,0:T(8,128)}, f32[20,8,128]{2,1,0:T(8,128)}, f32[4,256,128]{2,1,0:T(8,128)}, f32[4,16,128]{2,1,0:T(8,128)S(1)}) conditional(s32[]{:T(128)} %clamp.3, (f32[20,8,128]{2,1,0:T(8,128)S(1)}, s32[4]{0:T(128)S(1)}, f32[2,4,256,128]{3,2,1,0:T(8,128)S(1)}, f32[192,128]{1,0:T(8,128)S(1)}, ...), branch_computations={%region_0.1_spmd, %region_1.2_spmd, %region_2.3_spmd, %region_3.4_... | conditional | flops 8000000 | bytes 4655472 | solution.py:523
  23.3 1.9 %collective-permute-start.7 = (f32[20,8,128]{2,1,0:T(8,128)S(1)}, f32[20,8,128]{2,1,0:T(8,128)}, u32[]{:S(2)}, u32[]{:S(2)}) collective-permute-start(f32[20,8,128]{2,1,0:T(8,128)S(1)} %get-tuple-element.291), channel_id=1, source_target_pairs={{1,5},{3,3},{5,1},{7,31},{9,29},{11,27},{13,25},{15,23},{17,21},{1... | collective-permute-start | bytes 245768 | tf_op jit(solution)/shard_map/cond/branch_3_fun/ppermute | solution.py:498
  25.2 6.3 %collective-permute-start.6 = (f32[20,8,128]{2,1,0:T(8,128)S(1)}, f32[20,8,128]{2,1,0:T(8,128)}, u32[]{:S(2)}, u32[]{:S(2)}) collective-permute-start(f32[20,8,128]{2,1,0:T(8,128)S(1)} %get-tuple-element.291), channel_id=1, source_target_pairs={{1,7},{3,5},{5,3},{7,1},{9,31},{11,29},{13,27},{15,25},{17,23},{19... | collective-permute-start | bytes 245768 | tf_op jit(solution)/shard_map/cond/branch_3_fun/ppermute | solution.py:498
  31.6 3.4 %ends.19 = (f32[4,256,128]{2,1,0:T(8,128)}, f32[4,16,128]{2,1,0:T(8,128)S(1)}) custom-call(s32[4]{0:T(128)S(1)} %get-tuple-element.292.par, f32[2,4,256,128]{3,2,1,0:T(8,128)S(1)} %get-tuple-element.293.ends, f32[192,128]{1,0:T(8,128)S(1)} %get-tuple-element.294.g0, f32[192,128]{1,0:T(8,128)S(1)} %get-tuple-element.295.g1, ...), custom_call_target="tpu_custom_call" | custom-call | flops 8000000 | bytes 4000000 | tf_op jit(solution)/shard_map/cond/branch_3_fun/ends/pallas_call | solution.py:323
  35.0 0.0 collective-permute-done.7
  35.0 0.0 collective-permute-done.6
  35.0 0.0 collective-permute-done.34.ga
  35.0 0.0 copy-start.2
  35.0 0.6 %copy-done.2 = f32[20,8,128]{2,1,0:T(8,128)} copy-done((f32[20,8,128]{2,1,0:T(8,128)}, f32[20,8,128]{2,1,0:T(8,128)S(1)}, u32[]{:S(2)}) %copy-start.2) | copy-done | bytes 81944
  35.6 3.1 %band.1 = f32[4,256,128]{2,1,0:T(8,128)} custom-call(s32[4]{0:T(128)S(1)} %pad_add_fusion.par, f32[13,32,128]{2,1,0:T(8,128)} %get-tuple-element.433.edge, f32[7,32,128]{2,1,0:T(8,128)} %get-tuple-element.436.hedge, f32[20,8,128]{2,1,0:T(8,128)} %copy-done.2, f32[20,8,128]{2,1,0:T(8,128)} %get-tuple-element.441.gb, ...), custom_call_target="tpu_custom_call", output_to_operand_aliasing={{}: (7, {})} | custom-call | tf_op jit(solution)/shard_map/band/pallas_call | solution.py:447
Async XLA Ops:
  0.0 0.7 %copy-start.3 = (s32[128]{0:T(128)S(1)}, s32[128]{0:T(128)}, u32[]{:S(2)}) copy-start(s32[128]{0:T(128)} %param.32) | copy-start | bytes 1540
  5.1 4.7 %collective-permute-start.32 = (f32[192,128]{1,0:T(8,128)}, f32[192,128]{1,0:T(8,128)S(1)}, u32[]{:S(2)}, u32[]{:S(2)}) collective-permute-start(f32[192,128]{1,0:T(8,128)} %get-tuple-element.434), channel_id=1, source_target_pairs={{0,2},{1,3},{2,0},{3,1},{4,6},{5,7},{6,4},{7,5},{8,10},{9,11},{10,... | collective-permute-start | bytes 294920 | tf_op jit(solution)/shard_map/ppermute | solution.py:498
  5.2 7.2 %collective-permute-start.33 = (f32[192,128]{1,0:T(8,128)}, f32[192,128]{1,0:T(8,128)S(1)}, u32[]{:S(2)}, u32[]{:S(2)}) collective-permute-start(f32[192,128]{1,0:T(8,128)} %get-tuple-element.435), channel_id=1, source_target_pairs={{0,30},{1,31},{2,4},{3,5},{4,2},{5,3},{6,8},{7,9},{8,6},{9,7},{10,... | collective-permute-start | bytes 294920 | tf_op jit(solution)/shard_map/ppermute | solution.py:498
  12.4 2.5 %copy-start.1 = (f32[256,128]{1,0:T(8,128)S(1)}, f32[256,128]{1,0:T(8,128)}, u32[]{:S(2)}) copy-start(f32[256,128]{1,0:T(8,128)} %area.3) | copy-start | bytes 393220
  14.4 20.6 %collective-permute-start.34 = (f32[20,8,128]{2,1,0:T(8,128)}, f32[20,8,128]{2,1,0:T(8,128)S(1)}, u32[]{:S(2)}, u32[]{:S(2)}) collective-permute-start(f32[20,8,128]{2,1,0:T(8,128)} %get-tuple-element.437), channel_id=1, source_target_pairs={{0,1},{1,0},{2,3},{3,2},{4,5},{5,4},{6,7},{7,6},{8,9},{9,8},{10,11... | collective-permute-start | bytes 245768 | tf_op jit(solution)/shard_map/ppermute | solution.py:498
  14.9 8.4 %copy-start = (f32[4,256,128]{2,1,0:T(8,128)S(1)}, f32[4,256,128]{2,1,0:T(8,128)}, u32[]{:S(2)}) copy-start(f32[4,256,128]{2,1,0:T(8,128)} %param.33) | copy-start | bytes 1572868
  23.3 11.7 %collective-permute-start.7 = (f32[20,8,128]{2,1,0:T(8,128)S(1)}, f32[20,8,128]{2,1,0:T(8,128)}, u32[]{:S(2)}, u32[]{:S(2)}) collective-permute-start(f32[20,8,128]{2,1,0:T(8,128)S(1)} %get-tuple-element.291), channel_id=1, source_target_pairs={{1,5},{3,3},{5,1},{7,31},{9,29},{11,27},{13,25},{15,23},{17,21},{1... | collective-permute-start | bytes 245768 | tf_op jit(solution)/shard_map/cond/branch_3_fun/ppermute | solution.py:498
  25.2 9.8 %collective-permute-start.6 = (f32[20,8,128]{2,1,0:T(8,128)S(1)}, f32[20,8,128]{2,1,0:T(8,128)}, u32[]{:S(2)}, u32[]{:S(2)}) collective-permute-start(f32[20,8,128]{2,1,0:T(8,128)S(1)} %get-tuple-element.291), channel_id=1, source_target_pairs={{1,7},{3,5},{5,3},{7,1},{9,31},{11,29},{13,27},{15,25},{17,23},{19... | collective-permute-start | bytes 245768 | tf_op jit(solution)/shard_map/cond/branch_3_fun/ppermute | solution.py:498
  35.0 0.6 %copy-start.2 = (f32[20,8,128]{2,1,0:T(8,128)}, f32[20,8,128]{2,1,0:T(8,128)S(1)}, u32[]{:S(2)}) copy-start(f32[20,8,128]{2,1,0:T(8,128)S(1)} %collective-permute-done.34.ga) | copy-start | bytes 245764
